TPU v7x, 32 devices: a whole 2x2x4 slice. The times are simulated.
32 devices in a mesh: groups: 2 (over x), aux: 16 (over z, y, core).
Axes of the slice: x: 2, y: 2, z: 4, core: 2. Of those that a mesh axis runs over, the one named last changes fastest.
Arguments:
- coefficients: float32 [32, 256, 4096], P(('groups', 'aux')), parts along dimension 0, may hold values from -0.5 to 0.5
- screening: int32 [2, 32, 256], P(None, ('groups', 'aux')), parts along dimension 1, may hold values from 0 to 127, as said below
- kept_count: int32 [32], P(('groups', 'aux')), parts along dimension 0, may hold values from 1 to 256, 2048 in all
- occupied: float32 [16384, 125], P(('groups', 'aux')), parts along dimension 0, may hold values from -0.5 to 0.5
- owner_order: int32 [256], P('groups'), parts along dimension 0, may hold values from 0 to 127, each once
Outputs:
- k_panel: float32 [256, 64, 1024], P(('groups', 'aux')), parts along dimension 0
There are 2 independent parts, one for each index of `groups`. A program takes and returns all parts, laid end to end along the dimension named above; each array names one. Nothing has to cross between parts.
Inputs may be any that keep to these rules, and one draw needn't show every extreme that they name: Block indices of the screening list; the pairs of one auxiliary function are distinct. `kept_count`: the live slots of one part's 16 functions sum to 2048.
All inputs are finite; a program needn't handle non-finite values. No bound on the sum of `kept_count` on one device may be relied on, other than what follows from the above.
Results may differ from a plain program's by a relative error of at most 0.0003.
Values sent between devices are 32-bit elements; how exact they have to be, the bound alone decides.
A program may use at most 128 MiB of HBM per device.

v0:
```python
import jax
import jax.numpy as jnp
from jax import lax
from jax.sharding import PartitionSpec as P

BLK = 64
PBLK = 16


HIGHEST = lax.Precision.HIGHEST


def transform_slots(tile_values, col_blocks, row_blocks, live_mask, blocks, block_count):
    products = jnp.einsum("tmn,tni->tmi", tile_values, blocks[col_blocks], precision=HIGHEST)
    products = products * live_mask[:, None, None]
    return jax.ops.segment_sum(products, row_blocks, num_segments=block_count)


def shards(coefficients, screening, kept_count, occupied, owner_order):
    orbitals = lax.all_gather(occupied, "aux", axis=0, tiled=True)
    block_size = BLK
    slot_count = coefficients.shape[1]
    occ_count = orbitals.shape[1]
    block_count = orbitals.shape[0] // block_size
    blocks = orbitals.reshape(block_count, block_size, occ_count)
    tile_values = coefficients[0].reshape(slot_count, block_size, block_size)
    row_blocks = screening[0, 0]
    col_blocks = screening[1, 0]
    live_count = kept_count[0]
    live_mask = (jnp.arange(slot_count, dtype=jnp.int32) < live_count).astype(jnp.float32)
    half_done = transform_slots(tile_values, col_blocks, row_blocks, live_mask, blocks, block_count)
    ordered = half_done[owner_order]
    panel_width = PBLK * block_size
    panel_half = half_done[:PBLK].reshape(panel_width, occ_count)
    shard_count = lax.axis_size("aux")
    owned_blocks = block_count // shard_count
    owned_rows = owned_blocks * block_size
    grouped = ordered.reshape(1, shard_count, owned_blocks, block_size, occ_count)
    arrived = lax.all_to_all(grouped, "aux", split_axis=1, concat_axis=0, tiled=True)
    arrived = arrived.reshape(shard_count, owned_rows, occ_count)
    owned = jnp.einsum(
        "qri,qli->rl",
        arrived,
        lax.all_gather(panel_half.reshape(1, panel_width, occ_count), "aux", axis=0, tiled=True),
        precision=HIGHEST,
    )
    return owned.reshape(owned_blocks, block_size, panel_width)


def solution(mesh):
    return jax.shard_map(
        shards,
        mesh=mesh,
        in_specs=(
            P(("groups", "aux"), None, None),
            P(None, ("groups", "aux"), None),
            P(("groups", "aux")),
            P(("groups", "aux"), None),
            P("groups"),
        ),
        out_specs=P(("groups", "aux"), None, None),
        check_vma=False,
    )
```

profile of v0, /device:TPU:1, one launch (start us, length us, event | category | flops | bytes accessed | tf_op | source)
XLA Modules:
  0.0 301.2 jit_solution(612451229704961911)
XLA Ops:
  6.5 0.0 all-gather.3.cloned.1.call-start
  6.5 0.7 all-gather.3.cloned.1.call-update
  7.3 0.0 all-gather.5.cloned.1.call-start
  7.3 5.6 %copy.10 = f32[1,256,4096]{1,2,0:T(8,128)} copy(f32[1,256,4096]{2,1,0:T(8,128)} %param.5) | data formatting | bytes 8388608 | tf_op args[0]
  12.9 0.0 copy-start
  12.9 9.2 %copy.11 = f32[256,64,64]{2,1,0:T(8,128)} copy(f32[256,64,64]{0,2,1:T(8,128)} %bitcast.36) | data formatting | bytes 8388608 | tf_op jit(solution)/shard_map/reshape;squeeze | solution.py:26
  22.7 0.0 copy-done
  22.8 39.8 %all-gather.3.cloned.1.call-done = f32[8192,125]{1,0:T(8,128)} async-done(((f32[512,125]{1,0:T(8,128)}), f32[8192,125]{1,0:T(8,128)}) %all-gather.3.cloned.1.call-update) | async-done | bytes 4096016 | tf_op jit(solution)/shard_map/all_gather | solution.py:20
  62.6 6.5 %gather_fusion = f32[256,64,125]{2,1,0:T(8,128)} fusion(f32[128,64,125]{2,1,0:T(8,128)} %bitcast.37, s32[1024]{0:T(1024)S(1)} %pad_clamp_fusion.1), kind=kCustom, calls=%fused_computation | custom fusion | bytes 16385024 | tf_op jit(solution)/shard_map/gather | solution.py:14
  69.1 0.0 slice-start
  69.1 14.1 %multiply_bitcast_fusion = f32[256,64,125]{2,1,0:T(8,128)} fusion(f32[256]{0:T(256)S(1)} %compare_convert_fusion, f32[256,64,125]{2,1,0:T(8,128)} %gather_fusion, f32[256,64,64]{2,1,0:T(8,128)} %copy.11), kind=kOutput, calls=%fused_computation.5 | convolution fusion | flops 1574912000 | bytes 20579328 | tf_op jit(solution)/shard_map/tmn,tni->tmi/dot_general | solution.py:14
  83.2 2.5 broadcast_in_dim.8
  85.7 0.0 slice-done
  85.7 0.0 copy-start.1
  85.7 39.3 %scatter_fusion = f32[128,64,125]{2,1,0:T(8,128)} fusion(f32[128,64,125]{2,1,0:T(8,128)} %broadcast_in_dim.8, s32[256]{0:T(256)S(1)} %bitcast.40, f32[256,64,125]{2,1,0:T(8,128)} %multiply_bitcast_fusion), kind=kCustom, calls=%fused_computation.2 | custom fusion | flops 2048000 | bytes 24577024 | tf_op jit(solution)/shard_map/scatter-add | solution.py:16
  125.0 1.9 slice.16
  126.9 0.0 all-gather.5.cloned.1.call-update
  126.9 0.0 copy-done.1
  126.9 5.0 %gather_fusion.1 = f32[128,64,125]{2,1,0:T(8,128)} fusion(f32[128,64,125]{2,1,0:T(8,128)} %scatter_fusion, s32[1024]{0:T(1024)S(1)} %pad_clamp_fusion), kind=kCustom, calls=%fused_computation.1 | custom fusion | bytes 8192512 | tf_op jit(solution)/shard_map/gather | solution.py:32
  131.9 145.0 %all_to_all.4 = f32[1,16,8,64,125]{4,3,2,0,1:T(8,128)} all-to-all(f32[1,16,8,64,125]{4,3,2,0,1:T(8,128)} %bitcast.38), channel_id=1, replica_groups=mesh['groups'=2,'aux'=16] {'aux'}, dimensions={1} | all-to-all | bytes 8192000 | tf_op jit(solution)/shard_map/all_to_all | solution.py:39
  276.9 0.0 all-gather.5.cloned.1.call-done
  276.9 17.5 %fusion.3 = f32[8,64,1024]{2,1,0:T(8,128)} fusion(f32[16,1024,125]{2,1,0:T(8,128)} %all-gather.5.cloned.1.call-done, f32[1,16,8,64,125]{4,3,2,0,1:T(8,128)} %all_to_all.4), kind=kOutput, calls=%fused_computation.7 | convolution fusion | flops 12582912000 | bytes 14385152 | tf_op jit(solution)/shard_map/qri,qli->rl/dot_general | solution.py:41
  (5 shorter events, 0.0 us)
Async XLA Ops:
  6.5 56.1 %all-gather.3.cloned.1.call-start = ((), (), s32[]{:S(2)}) async-start(), calls=%async_computation.1 | async-start | bytes 4456448 | tf_op jit(solution)/shard_map/all_gather | solution.py:20
  7.3 269.6 %all-gather.5.cloned.1.call-start = ((), (), s32[]{:S(2)}) async-start(), calls=%async_computation.2 | async-start | bytes 8912896 | tf_op jit(solution)/shard_map/all_gather | solution.py:44
  12.9 9.8 %copy-start = (s32[2,1,256]{2,1,0:T(1,128)S(1)}, s32[2,1,256]{2,1,0:T(1,128)}, u32[]{:S(2)}) copy-start(s32[2,1,256]{2,1,0:T(1,128)} %param.6) | copy-start | bytes 6148
  69.1 16.5 %slice-start = ((s32[2,1,256]{2,1,0:T(1,128)}), s32[1,1,256]{2,1,0:T(1,128)S(1)}, s32[]{:S(2)}) async-start(s32[2,1,256]{2,1,0:T(1,128)} %param.6), calls=%async_computation.3 | async-start | bytes 2048 | tf_op jit(solution)/shard_map/slice | solution.py:27
  85.7 41.2 %copy-start.1 = (s32[128]{0:T(128)S(1)}, s32[128]{0:T(128)}, u32[]{:S(2)}) copy-start(s32[128]{0:T(128)} %param.9) | copy-start | bytes 1540
Sparse Core Ops, SparseCore 0:
  9.5 53.0 all-gather.2
  127.0 134.5 all-gather.4
where the time goes:
time: 302 us; the launch traced here: 301 us
  blocking collectives  145 us (48%)
  waiting for transfers between devices  40.6 us (13%)
  other arithmetic  39.3 us (13%)
  matrix products  31.5 us (10%)
  local copies, waits for them, and re-layouts  30.6 us (10%)
  between operations  14.1 us (5%)
    all_to_all x1, blocking collectives, shards(): lax.all_to_all(grouped, 'aux', split_axis=1, concat_axis=0, tiled=True)  145 us
    all_gather x1, waiting for transfers between devices, shards(): orbitals = lax.all_gather(occupied, 'aux', axis=0, tiled=True)  39.8 us
    scatter-add x1, other arithmetic, transform_slots(): return jax.ops.segment_sum(products, row_blocks, num_segments=block_count)  39.3 us
    dot_general x1, matrix products, shards(): jnp.einsum('qri,qli->rl', arrived, lax.all_gather(panel_half.reshape(1, p...  17.5 us
    dot_general x1, matrix products, transform_slots(): jnp.einsum('tmn,tni->tmi', tile_values, blocks[col_blocks], precision=HIG...  14.1 us
    another operation x1, local copies, waits for them, and re-layouts, shards(): tile_values = coefficients[0].reshape(slot_count, block_size, block_size)  9.16 us
    gather x1, local copies, waits for them, and re-layouts, transform_slots(): blocks[col_blocks]  6.51 us
  transfers between devices with their start and end apart: 2, of which 1 were waited for; matrix products, arithmetic and copies ran while one was open for 7% of the time, Pallas kernels for 0%

commit v1 on v0

v1 whole, which is shorter than its diff:
```python
import functools

import jax
import jax.numpy as jnp
from jax import lax
from jax.experimental import pallas as pl
from jax.experimental.pallas import tpu as pltpu
from jax.sharding import PartitionSpec as P

BLK = 64
PBLK = 16
LANES = 128
GROUP = 8
TILE = 256
VMEM_BYTES = 56 * 2**20
MESH_ID = pl.DeviceIdType.MESH


def halves(x):
    high = x.astype(jnp.bfloat16)
    low = (x - high.astype(jnp.float32)).astype(jnp.bfloat16)
    return high, low


def half_kernel(block_count, occ, kept_ref, rows_ref, cols_ref, place_ref, tiles_ref, orbitals_ref, half_ref, panel_ref, weights):
    @pl.loop(0, block_count)
    def _(b):
        high, low = halves(orbitals_ref[b])
        pad = jnp.zeros((BLK, LANES - occ), jnp.bfloat16)
        high = jnp.concatenate([high, pad], axis=1)
        low = jnp.concatenate([low, pad], axis=1)
        weights[b] = jnp.concatenate([high, high, low, low], axis=0)
        half_ref[b] = jnp.zeros((BLK, LANES), jnp.float32)

    half_ref[block_count] = jnp.zeros((BLK, LANES), jnp.float32)
    live = kept_ref[0]

    @pl.loop(0, (live + GROUP - 1) // GROUP)
    def _(g):
        products = []
        for u in range(GROUP):
            t = g * GROUP + u
            tile = tiles_ref[t]
            lhs = jnp.concatenate([tile, tile], axis=1)
            products.append(jnp.dot(lhs, weights[cols_ref[t]], preferred_element_type=jnp.float32))
        for u in range(GROUP):
            t = g * GROUP + u
            place = jnp.where(t < live, place_ref[rows_ref[t]], block_count)
            half_ref[place] += products[u]

    for a in range(PBLK):
        panel_ref[pl.ds(a * BLK, BLK), :] = half_ref[place_ref[a]]


def exchange_kernel(shape, half_ref, panel_ref, out_ref, arrived, panels, lhs, a_send, a_recv, z_send, y_send, c_send, p_recv, local_sem):
    nz, ny, n = shape
    owned = arrived.shape[1]
    me = lax.axis_index("aux")
    z, y, c = me // (2 * ny), (me // 2) % ny, me % 2

    def index(zz, yy, cc):
        return (zz * ny + yy) * 2 + cc

    def partner(i):
        k = lax.rem(i // (2 * ny) + nz // 2, nz)
        return k, lax.rem(i // 2, ny), lax.rem(i, 2)

    def send_to(i):
        k, dy, dc = partner(i)
        return index(lax.rem(z + k, nz), lax.rem(y + dy, ny), lax.rem(c + dc, 2))

    def recv_from(i):
        k, dy, dc = partner(i)
        return index(lax.rem(z - k + nz, nz), lax.rem(y - dy + ny, ny), lax.rem(c - dc + 2, 2))

    barrier = pltpu.get_barrier_semaphore()

    @pl.loop(1, n)
    def _(k):
        pl.semaphore_signal(barrier, inc=1, device_id={"aux": lax.rem(me + k, n)}, device_id_type=MESH_ID)

    pl.semaphore_wait(barrier, n - 1)

    def panel_copy(q, dst, sem, own=False):
        return pltpu.make_async_remote_copy(
            src_ref=panel_ref if own else panels.at[q],
            dst_ref=panels.at[q],
            send_sem=sem,
            recv_sem=p_recv.at[q],
            device_id={"aux": dst},
            device_id_type=MESH_ID,
        )

    def row_copy(dst, slot):
        return pltpu.make_async_remote_copy(
            src_ref=half_ref.at[pl.ds(dst * owned, owned)],
            dst_ref=arrived.at[slot],
            send_sem=a_send.at[dst],
            recv_sem=a_recv.at[slot],
            device_id={"aux": dst},
            device_id_type=MESH_ID,
        )

    def wait_panel(q):
        panel_copy(q, me, c_send.at[q]).wait_recv()

    up, down = index(z + 1, y, c), index(z - 1, y, c)
    other_y, other_c = index(z, ny - 1 - y, c), index(z, y, 1 - c)

    def spread(q, own=False):
        if ny > 1:
            panel_copy(q, other_y, y_send.at[q], own).start()
        panel_copy(q, other_c, c_send.at[q], own).start()

    @pl.when(z < nz - 1)
    def _():
        panel_copy(me, up, z_send.at[0, me], True).start()

    @pl.when(z > 0)
    def _():
        panel_copy(me, down, z_send.at[1, me], True).start()

    spread(me, True)
    own_panel = pltpu.make_async_copy(panel_ref, panels.at[me], local_sem.at[0])
    own_rows = pltpu.make_async_copy(half_ref.at[pl.ds(me * owned, owned)], arrived.at[me], local_sem.at[1])
    own_panel.start()
    own_rows.start()

    @pl.loop(0, n)
    def _(i):
        dst = send_to(i)

        @pl.when(dst != me)
        def _():
            row_copy(dst, me).start()

    def from_y(zz):
        if ny > 1:
            q = index(zz, ny - 1 - y, c)
            wait_panel(q)
            panel_copy(q, other_c, c_send.at[q]).start()

    from_y(z)

    @pl.loop(1, nz)
    def _(d):
        @pl.when(z - d >= 0)
        def _():
            q = index(z - d, y, c)
            wait_panel(q)

            @pl.when(z < nz - 1)
            def _():
                panel_copy(q, up, z_send.at[0, q]).start()

            spread(q)

        @pl.when(z + d < nz)
        def _():
            q = index(z + d, y, c)
            wait_panel(q)

            @pl.when(z > 0)
            def _():
                panel_copy(q, down, z_send.at[1, q]).start()

            spread(q)

        @pl.when(z - d >= 0)
        def _():
            from_y(z - d)

        @pl.when(z + d < nz)
        def _():
            from_y(z + d)

    @pl.loop(0, nz * ny)
    def _(j):
        wait_panel(2 * j + 1 - c)

    own_panel.wait()
    own_rows.wait()
    out_ref[...] = jnp.zeros_like(out_ref)
    rows = owned * BLK
    width = out_ref.shape[1]

    @pl.loop(0, n)
    def _(i):
        q = recv_from(i)

        @pl.when(q != me)
        def _():
            row_copy(me, q).wait_recv()

        high, low = halves(arrived[q].reshape(rows, LANES))
        lhs[...] = jnp.concatenate([high, high, low], axis=1)

        @pl.loop(0, width // TILE)
        def _(j):
            start = pl.multiple_of(j * TILE, TILE)
            p_high, p_low = halves(panels[q, pl.ds(start, TILE), :])
            rhs = jnp.concatenate([p_high, p_low, p_high], axis=1)
            out_ref[:, pl.ds(start, TILE)] += lax.dot_general(
                lhs[...], rhs, (((1,), (1,)), ((), ())), preferred_element_type=jnp.float32
            )

    @pl.loop(0, n)
    def _(i):
        dst = send_to(i)

        @pl.when(dst != me)
        def _():
            row_copy(dst, me).wait_send()

    @pl.loop(0, nz)
    def _(zz):
        q = index(zz, y, c)

        @pl.when((zz <= z) & (z < nz - 1))
        def _():
            panel_copy(q, up, z_send.at[0, q]).wait_send()

        @pl.when((zz >= z) & (z > 0))
        def _():
            panel_copy(q, down, z_send.at[1, q]).wait_send()

        if ny > 1:
            panel_copy(q, other_y, y_send.at[q]).wait_send()

    @pl.loop(0, nz * ny)
    def _(j):
        q = 2 * j + c
        panel_copy(q, other_c, c_send.at[q]).wait_send()


def shards(coefficients, screening, kept_count, occupied, owner_order):
    slot_count = coefficients.shape[1]
    occ = occupied.shape[1]
    n = lax.axis_size("aux")
    orbitals = lax.all_gather(occupied, "aux", axis=0, tiled=True)
    block_count = orbitals.shape[0] // BLK
    owned = block_count // n
    width = PBLK * BLK
    high, low = halves(coefficients[0].reshape(slot_count, BLK, BLK))
    tiles = jnp.concatenate([high, low], axis=-1)
    place = jnp.zeros((block_count,), jnp.int32).at[owner_order].set(jnp.arange(block_count, dtype=jnp.int32))
    smem = pl.BlockSpec(memory_space=pltpu.SMEM)
    vmem = pl.BlockSpec(memory_space=pltpu.VMEM)
    anyw = pl.BlockSpec(memory_space=pl.ANY)
    half, panel = pl.pallas_call(
        functools.partial(half_kernel, block_count, occ),
        out_shape=(
            jax.ShapeDtypeStruct((block_count + 1, BLK, LANES), jnp.float32),
            jax.ShapeDtypeStruct((width, LANES), jnp.float32),
        ),
        in_specs=[smem] * 4 + [vmem] * 2,
        out_specs=(vmem, vmem),
        scratch_shapes=[pltpu.VMEM((block_count, 4 * BLK, LANES), jnp.bfloat16)],
        compiler_params=pltpu.CompilerParams(vmem_limit_bytes=VMEM_BYTES),
    )(kept_count, screening[0, 0], screening[1, 0], place, tiles, orbitals.reshape(block_count, BLK, occ))

    ny = 2 if n == 16 else 1
    nz = n // (2 * ny)
    dma = pltpu.SemaphoreType.DMA
    rows = owned * BLK
    out = pl.pallas_call(
        functools.partial(exchange_kernel, (nz, ny, n)),
        out_shape=jax.ShapeDtypeStruct((rows, width), jnp.float32),
        in_specs=[anyw, anyw],
        out_specs=vmem,
        scratch_shapes=[
            pltpu.VMEM((n, owned, BLK, LANES), jnp.float32),
            pltpu.VMEM((n, width, LANES), jnp.float32),
            pltpu.VMEM((rows, 3 * LANES), jnp.bfloat16),
            dma((n,)), dma((n,)), dma((2, n)), dma((n,)), dma((n,)), dma((n,)), dma((2,)),
        ],
        compiler_params=pltpu.CompilerParams(collective_id=0, has_side_effects=True, vmem_limit_bytes=VMEM_BYTES),
    )(half, panel)
    return out.reshape(owned, BLK, width)


def solution(mesh):
    return jax.shard_map(
        shards,
        mesh=mesh,
        in_specs=(
            P(("groups", "aux"), None, None),
            P(None, ("groups", "aux"), None),
            P(("groups", "aux")),
            P(("groups", "aux"), None),
            P("groups"),
        ),
        out_specs=P(("groups", "aux"), None, None),
        check_vma=False,
    )
```

time: 302 us -> 256 us (0.85)
  Pallas kernels: 0 us -> 183 us
  blocking collectives: 145 us -> 0 us
  matrix products: 31.5 us -> 0 us
  other arithmetic: 39.3 us -> 12.3 us
  waiting for transfers between devices: 40.6 us -> 19.7 us
  local copies, waits for them, and re-layouts: 30.6 us -> 26.6 us
    pallas_call x0 -> x2, Pallas kernels: none -> 183 us  [the longest x1 171 us: shards(): pl.pallas_call(functools.partial(exchange_kernel, (nz, ny, n)), out_shape...]
    all_to_all x1 -> x0, blocking collectives: 145 us -> none  [shards(): lax.all_to_all(grouped, 'aux', split_axis=1, concat_axis=0, tiled=True)]
    scatter-add x1 -> x0, other arithmetic: 39.3 us -> none  [transform_slots(): return jax.ops.segment_sum(products, row_blocks, num_segments=block_count)]
    dot_general x2 -> x0, matrix products: 31.5 us -> none  [the longest x1 17.5 us: shards(): jnp.einsum('qri,qli->rl', arrived, lax.all_gather(panel_half.reshape(1, p...]
    all_gather x1, waiting for transfers between devices: 39.8 us -> 19 us  [shards(): orbitals = lax.all_gather(occupied, 'aux', axis=0, tiled=True)]
    gather x2 -> x0, local copies, waits for them, and re-layouts: 11.5 us -> none  [the longest x1 6.51 us: transform_slots(): blocks[col_blocks]]
    convert_element_type x1 -> x2, other arithmetic: 0.01 us -> 8.61 us  [the longest x1 6.12 us: halves(): low = (x - high.astype(jnp.float32)).astype(jnp.bfloat16)]
    convert_element_type x0 -> x1, local copies, waits for them, and re-layouts: none -> 6.64 us  [halves(): high = x.astype(jnp.bfloat16)]
  transfers between devices with their start and end apart: 2 -> 1, of which waited for: 1 -> 1; matrix products, arithmetic and copies ran while one was open for 7% -> 14% of each run, Pallas kernels for 0% -> 0%
where the time goes in v1:
time: 256 us
  Pallas kernels  183 us (71%)
  local copies, waits for them, and re-layouts  26.6 us (10%)
  waiting for transfers between devices  19.7 us (8%)
  between operations  14.1 us (6%)
  other arithmetic  12.3 us (5%)
    pallas_call x1, Pallas kernels, shards(): pl.pallas_call(functools.partial(exchange_kernel, (nz, ny, n)), out_shape...  171 us
    all_gather x1, waiting for transfers between devices, shards(): orbitals = lax.all_gather(occupied, 'aux', axis=0, tiled=True)  19 us
    pallas_call x1, Pallas kernels, shards(): pl.pallas_call(functools.partial(half_kernel, block_count, occ), out_shap...  11.3 us
    another operation x1, local copies, waits for them, and re-layouts, shards(): high, low = halves(coefficients[0].reshape(slot_count, BLK, BLK))  9.16 us
    unnamed x8, local copies, waits for them, and re-layouts  8.79 us
    convert_element_type x1, local copies, waits for them, and re-layouts, halves(): high = x.astype(jnp.bfloat16)  6.64 us
    convert_element_type x1, other arithmetic, halves(): low = (x - high.astype(jnp.float32)).astype(jnp.bfloat16)  6.12 us
  transfers between devices with their start and end apart: 1, of which 1 were waited for; matrix products, arithmetic and copies ran while one was open for 14% of the time, Pallas kernels for 0%

profile of v1, /device:TPU:1, one launch (start us, length us, event | category | flops | bytes accessed | tf_op | source)
XLA Modules:
  0.0 255.5 jit_solution(17750851557883759079)
XLA Ops:
  6.5 0.0 all-gather.2.cloned.1.call-start
  6.5 0.7 all-gather.2.cloned.1.call-update
  7.3 5.6 %copy.9 = f32[1,256,4096]{1,2,0:T(8,128)} copy(f32[1,256,4096]{2,1,0:T(8,128)} %param.5) | data formatting | bytes 8388608 | tf_op args[0]
  12.9 2.5 convert_element_type.9
  15.4 9.2 %copy.11 = f32[256,64,64]{2,1,0:T(8,128)} copy(f32[256,64,64]{0,2,1:T(8,128)} %bitcast.6) | data formatting | bytes 8388608 | tf_op jit(solution)/shard_map/reshape;squeeze | solution.py:244
  24.5 0.0 copy-start.2
  24.5 6.6 %copy.12 = bf16[256,64,64]{2,1,0:T(8,128)(2,1)} copy(bf16[256,64,64]{0,2,1:T(8,128)(2,1)S(1)} %convert_element_type.9) | data formatting | bytes 4194304 | tf_op jit(solution)/shard_map/convert_element_type | solution.py:20
  31.8 0.0 copy-done.2
  31.9 1.5 scatter_custom_fusion.place_ref
  33.3 0.0 copy-start
  33.3 6.1 %subtract_convert_fusion = bf16[256,64,64]{2,1,0:T(8,128)(2,1)S(1)} fusion(f32[256,64,64]{2,1,0:T(8,128)} %copy.11, bf16[256,64,64]{2,1,0:T(8,128)(2,1)} %copy.12), kind=kLoop, calls=%fused_computation.1 | loop fusion | flops 3145728 | bytes 8388608 | tf_op jit(solution)/shard_map/convert_element_type | solution.py:21
  39.5 0.0 copy-done
  39.5 0.0 copy-start.1
  39.5 3.7 %pad_maximum_fusion.tiles_ref = bf16[256,64,128]{2,1,0:T(8,128)(2,1)} fusion(bf16[256,64,64]{2,1,0:T(8,128)(2,1)S(1)} %subtract_convert_fusion, bf16[256,64,64]{2,1,0:T(8,128)(2,1)S(1)} %copy-done), kind=kLoop, calls=%fused_computation.2 | loop fusion | flops 8388608 | bytes 8388608 | tf_op jit(solution)/shard_map/concatenate | solution.py:245
  43.2 0.0 copy-done.1
  43.2 0.6 fusion.2
  43.7 19.0 %all-gather.2.cloned.1.call-done = f32[8192,125]{1,0:T(8,128)} async-done(((f32[512,125]{1,0:T(8,128)}), f32[8192,125]{1,0:T(8,128)}) %all-gather.2.cloned.1.call-update) | async-done | bytes 4096016 | tf_op jit(solution)/shard_map/all_gather | solution.py:240
  62.8 11.3 %shard_map.55 = (f32[129,64,128]{2,1,0:T(8,128)}, f32[1024,128]{1,0:T(8,128)}) custom-call(s32[1]{0:T(128)S(6)} %copy.14.kept_ref, s32[256]{0:T(256)} %bitcast.10, s32[256]{0:T(256)} %bitcast.9, s32[128]{0:T(128)} %scatter_custom_fusion.place_ref, bf16[256,64,128]{2,1,0:T(8,128)(2,1)} %pad_maximum_fusion.tiles_ref, f32[128,64,125]{2,1,0:T(8,128)} %bitcast.8), custom_call_target="tpu_custom_call" | custom-call | tf_op jit(solution)/shard_map/pallas_call | solution.py:250
  74.0 171.5 %shard_map.56 = f32[512,1024]{1,0:T(8,128)} custom-call(f32[129,64,128]{2,1,0:T(8,128)} %get-tuple-element.7.half_ref, f32[1024,128]{1,0:T(8,128)} %get-tuple-element.8.panel_ref), custom_call_target="tpu_custom_call" | custom-call | tf_op jit(solution)/shard_map/pallas_call | solution.py:266
  245.5 3.2 %copy.15 = f32[8,64,1024]{2,1,0:T(8,128)} copy(f32[8,64,1024]{2,1,0:T(8,128)} %bitcast.7) | data formatting | bytes 4194304
  (2 shorter events, 0.0 us)
Async XLA Ops:
  6.5 56.2 %all-gather.2.cloned.1.call-start = ((), (), s32[]{:S(2)}) async-start(), calls=%async_computation | async-start | bytes 4456448 | tf_op jit(solution)/shard_map/all_gather | solution.py:240
  24.5 7.3 %copy-start.2 = (s32[128]{0:T(128)S(1)}, s32[128]{0:T(128)}, u32[]{:S(2)}) copy-start(s32[128]{0:T(128)} %param.9) | copy-start | bytes 1540
  33.3 6.1 %copy-start = (bf16[256,64,64]{2,1,0:T(8,128)(2,1)S(1)}, bf16[256,64,64]{2,1,0:T(8,128)(2,1)}, u32[]{:S(2)}) copy-start(bf16[256,64,64]{2,1,0:T(8,128)(2,1)} %copy.12) | copy-start | bytes 6291460
  39.5 3.7 %copy-start.1 = (s32[2,1,256]{2,1,0:T(1,128)S(1)}, s32[2,1,256]{2,1,0:T(1,128)}, u32[]{:S(2)}) copy-start(s32[2,1,256]{2,1,0:T(1,128)} %param.6) | copy-start | bytes 6148
Sparse Core Ops, SparseCore 0:
  9.5 53.2 all-gather.1

commit v2 on v1

--- a/solution.py
+++ b/solution.py
@@ -22,13 +22,10 @@
     return high, low
 
 
-def half_kernel(block_count, occ, kept_ref, rows_ref, cols_ref, place_ref, tiles_ref, orbitals_ref, half_ref, panel_ref, weights):
+def half_kernel(block_count, kept_ref, rows_ref, cols_ref, place_ref, tiles_ref, orbitals_ref, half_ref, panel_ref, weights):
     @pl.loop(0, block_count)
     def _(b):
         high, low = halves(orbitals_ref[b])
-        pad = jnp.zeros((BLK, LANES - occ), jnp.bfloat16)
-        high = jnp.concatenate([high, pad], axis=1)
-        low = jnp.concatenate([low, pad], axis=1)
         weights[b] = jnp.concatenate([high, high, low, low], axis=0)
         half_ref[b] = jnp.zeros((BLK, LANES), jnp.float32)
 
@@ -46,10 +43,148 @@
         for u in range(GROUP):
             t = g * GROUP + u
             place = jnp.where(t < live, place_ref[rows_ref[t]], block_count)
-            half_ref[place] += products[u]
+            for parity in range(2):
+                part = products[u][parity * (BLK // 2):(parity + 1) * (BLK // 2)]
+                half_ref[place, pl.ds(parity, BLK // 2, stride=2), :] += part
 
     for a in range(PBLK):
         panel_ref[pl.ds(a * BLK, BLK), :] = half_ref[place_ref[a]]
+
+
+def spread_kernel(shape, coefficients_ref, shard_ref, tiles_ref, gathered, z_send, y_send, c_send, recv, local_sem):
+    nz, ny, n = shape
+    me = lax.axis_index("aux")
+    z, y, c = me // (2 * ny), (me // 2) % ny, me % 2
+
+    def index(zz, yy, cc):
+        return (zz * ny + yy) * 2 + cc
+
+    barrier = pltpu.get_barrier_semaphore()
+
+    @pl.loop(1, n)
+    def _(k):
+        pl.semaphore_signal(barrier, inc=1, device_id={"aux": lax.rem(me + k, n)}, device_id_type=MESH_ID)
+
+    pl.semaphore_wait(barrier, n - 1)
+
+    def copy(q, dst, sem, own=False):
+        return pltpu.make_async_remote_copy(
+            src_ref=shard_ref if own else gathered.at[q],
+            dst_ref=gathered.at[q],
+            send_sem=sem,
+            recv_sem=recv.at[q],
+            device_id={"aux": dst},
+            device_id_type=MESH_ID,
+        )
+
+    up, down = index(z + 1, y, c), index(z - 1, y, c)
+    other_y, other_c = index(z, ny - 1 - y, c), index(z, y, 1 - c)
+
+    def wait(q):
+        copy(q, other_c, c_send.at[q]).wait_recv()
+
+    def spread(q, own=False):
+        if ny > 1:
+            copy(q, other_y, y_send.at[q], own).start()
+        copy(q, other_c, c_send.at[q], own).start()
+
+    @pl.when(z < nz - 1)
+    def _():
+        copy(me, up, z_send.at[0, me], True).start()
+
+    @pl.when(z > 0)
+    def _():
+        copy(me, down, z_send.at[1, me], True).start()
+
+    spread(me, True)
+    own_shard = pltpu.make_async_copy(shard_ref, gathered.at[me], local_sem)
+    own_shard.start()
+
+    slots = tiles_ref.shape[0] // nz
+    group = min(GROUP, slots)
+
+    def prepare(part):
+        @pl.loop(0, slots // group)
+        def _(g):
+            for u in range(group):
+                t = part * slots + g * group + u
+                tile = coefficients_ref[t]
+                high = tile.astype(jnp.bfloat16).astype(jnp.float32)
+                low = tile - high
+                first = lax.broadcasted_iota(jnp.int32, tile.shape, 1) < BLK
+                even = jnp.where(first, high, pltpu.roll(low, BLK, 1))
+                odd = jnp.where(first, pltpu.roll(high, BLK, 1), low)
+                tiles_ref[t] = jnp.concatenate([even, odd], axis=0).astype(jnp.bfloat16)
+
+    def from_y(zz):
+        if ny > 1:
+            q = index(zz, ny - 1 - y, c)
+            wait(q)
+            copy(q, other_c, c_send.at[q]).start()
+
+    prepare(0)
+
+    @pl.loop(1, nz)
+    def _(d):
+        @pl.when(z - d >= 0)
+        def _():
+            q = index(z - d, y, c)
+            wait(q)
+
+            @pl.when(z < nz - 1)
+            def _():
+                copy(q, up, z_send.at[0, q]).start()
+
+            spread(q)
+
+        @pl.when(z + d < nz)
+        def _():
+            q = index(z + d, y, c)
+            wait(q)
+
+            @pl.when(z > 0)
+            def _():
+                copy(q, down, z_send.at[1, q]).start()
+
+            spread(q)
+
+        prepare(d)
+
+    @pl.loop(0, nz)
+    def _(d):
+        @pl.when(z - d >= 0)
+        def _():
+            from_y(z - d)
+
+        @pl.when((z + d < nz) & (d > 0))
+        def _():
+            from_y(z + d)
+
+    @pl.loop(0, nz * ny)
+    def _(j):
+        wait(2 * j + 1 - c)
+
+    own_shard.wait()
+
+    @pl.loop(0, nz)
+    def _(zz):
+        q = index(zz, y, c)
+
+        @pl.when((zz <= z) & (z < nz - 1))
+        def _():
+            copy(q, up, z_send.at[0, q]).wait_send()
+
+        @pl.when((zz >= z) & (z > 0))
+        def _():
+            copy(q, down, z_send.at[1, q]).wait_send()
+
+        if ny > 1:
+            copy(q, other_y, y_send.at[q]).wait_send()
+
+    @pl.loop(0, nz * ny)
+    def _(j):
+        q = 2 * j + c
+        copy(q, other_c, c_send.at[q]).wait_send()
 
 
 def exchange_kernel(shape, half_ref, panel_ref, out_ref, arrived, panels, lhs, a_send, a_recv, z_send, y_send, c_send, p_recv, local_sem):
@@ -237,18 +372,31 @@
     slot_count = coefficients.shape[1]
     occ = occupied.shape[1]
     n = lax.axis_size("aux")
-    orbitals = lax.all_gather(occupied, "aux", axis=0, tiled=True)
-    block_count = orbitals.shape[0] // BLK
+    shard_rows = occupied.shape[0]
+    block_count = shard_rows * n // BLK
     owned = block_count // n
     width = PBLK * BLK
-    high, low = halves(coefficients[0].reshape(slot_count, BLK, BLK))
-    tiles = jnp.concatenate([high, low], axis=-1)
+    ny = 2 if n == 16 else 1
+    nz = n // (2 * ny)
+    dma = pltpu.SemaphoreType.DMA
     place = jnp.zeros((block_count,), jnp.int32).at[owner_order].set(jnp.arange(block_count, dtype=jnp.int32))
     smem = pl.BlockSpec(memory_space=pltpu.SMEM)
     vmem = pl.BlockSpec(memory_space=pltpu.VMEM)
     anyw = pl.BlockSpec(memory_space=pl.ANY)
+    flat = BLK * BLK // LANES
+    tiles, orbitals = pl.pallas_call(
+        functools.partial(spread_kernel, (nz, ny, n)),
+        out_shape=(
+            jax.ShapeDtypeStruct((slot_count, BLK, LANES), jnp.bfloat16),
+            jax.ShapeDtypeStruct((n, shard_rows, LANES), jnp.float32),
+        ),
+        in_specs=[vmem, anyw],
+        out_specs=(vmem, anyw),
+        scratch_shapes=[dma((2, n)), dma((n,)), dma((n,)), dma((n,)), dma],
+        compiler_params=pltpu.CompilerParams(collective_id=1, has_side_effects=True, vmem_limit_bytes=VMEM_BYTES),
+    )(coefficients[0].reshape(slot_count, flat, LANES), jnp.pad(occupied, ((0, 0), (0, LANES - occ))))
     half, panel = pl.pallas_call(
-        functools.partial(half_kernel, block_count, occ),
+        functools.partial(half_kernel, block_count),
         out_shape=(
             jax.ShapeDtypeStruct((block_count + 1, BLK, LANES), jnp.float32),
             jax.ShapeDtypeStruct((width, LANES), jnp.float32),
@@ -257,11 +405,8 @@
         out_specs=(vmem, vmem),
         scratch_shapes=[pltpu.VMEM((block_count, 4 * BLK, LANES), jnp.bfloat16)],
         compiler_params=pltpu.CompilerParams(vmem_limit_bytes=VMEM_BYTES),
-    )(kept_count, screening[0, 0], screening[1, 0], place, tiles, orbitals.reshape(block_count, BLK, occ))
-
-    ny = 2 if n == 16 else 1
-    nz = n // (2 * ny)
-    dma = pltpu.SemaphoreType.DMA
+    )(kept_count, screening[0, 0], screening[1, 0], place, tiles, orbitals.reshape(block_count, BLK, LANES))
+
     rows = owned * BLK
     out = pl.pallas_call(
         functools.partial(exchange_kernel, (nz, ny, n)),

time: 256 us -> 236 us (0.922)
  Pallas kernels: 183 us -> 222 us
  waiting for transfers between devices: 19.7 us -> 0 us
  local copies, waits for them, and re-layouts: 26.6 us -> 12.4 us
  between operations: 14.1 us -> 0.67 us
  other arithmetic: 12.3 us -> 0.66 us
    pallas_call x1 -> x2, Pallas kernels: 11.3 us -> 54 us  [the longest x1 39.9 us: shards(): pl.pallas_call(functools.partial(spread_kernel, (nz, ny, n)), out_shape=(...]
    all_gather x1 -> x0, waiting for transfers between devices: 19 us -> none  [shards(): orbitals = lax.all_gather(occupied, 'aux', axis=0, tiled=True)]
    another operation x1 -> x0, local copies, waits for them, and re-layouts: 9.16 us -> none  [shards(): high, low = halves(coefficients[0].reshape(slot_count, BLK, BLK))]
    convert_element_type x2 -> x0, other arithmetic: 8.61 us -> none  [the longest x1 6.12 us: halves(): low = (x - high.astype(jnp.float32)).astype(jnp.bfloat16)]
    convert_element_type x1 -> x0, local copies, waits for them, and re-layouts: 6.64 us -> none  [halves(): high = x.astype(jnp.bfloat16)]
    concatenate x1 -> x0, other arithmetic: 3.67 us -> none  [shards(): tiles = jnp.concatenate([high, low], axis=-1)]
    pallas_call x1, Pallas kernels: 171 us -> 168 us  [shards(): pl.pallas_call(functools.partial(exchange_kernel, (nz, ny, n)), out_shape...]
    unnamed x8 -> x2, local copies, waits for them, and re-layouts: 8.79 us -> 8.03 us
  transfers between devices with their start and end apart: 1 -> 0, of which waited for: 1 -> 0; matrix products, arithmetic and copies ran while one was open for 14% -> 0% of each run, Pallas kernels for 0% -> 0%
where the time goes in v2:
time: 236 us
  Pallas kernels  222 us (94%)
  local copies, waits for them, and re-layouts  12.4 us (5%)
    pallas_call x1, Pallas kernels, shards(): pl.pallas_call(functools.partial(exchange_kernel, (nz, ny, n)), out_shape...  168 us
    pallas_call x1, Pallas kernels, shards(): pl.pallas_call(functools.partial(spread_kernel, (nz, ny, n)), out_shape=(...  39.9 us
    pallas_call x1, Pallas kernels, shards(): pl.pallas_call(functools.partial(half_kernel, block_count), out_shape=(ja...  14.1 us
    unnamed x2, local copies, waits for them, and re-layouts  8.03 us

profile of v2, /device:TPU:1, one launch (start us, length us, event | category | flops | bytes accessed | tf_op | source)
XLA Modules:
  0.0 235.7 jit_solution(10613614450433194666)
XLA Ops:
  0.7 0.7 compare_select_fusion
  1.3 1.4 scatter_custom_fusion.place_ref
  2.8 1.2 fusion.2
  4.0 1.7 pad.4.shard_ref
  5.7 4.9 %copy.6 = f32[32,8,32,128]{3,2,1,0:T(8,128)} copy(f32[32,8,32,128]{3,1,2,0:T(8,128)} %bitcast.11) | data formatting | bytes 8388608
  10.5 39.9 %shard_map.55 = (bf16[256,64,128]{2,1,0:T(8,128)(2,1)}, f32[16,512,128]{2,1,0:T(8,128)}) custom-call(f32[256,32,128]{2,1,0:T(8,128)} %bitcast.8, f32[512,128]{1,0:T(8,128)} %pad.4.shard_ref), custom_call_target="tpu_custom_call" | custom-call | tf_op jit(solution)/shard_map/pallas_call | solution.py:387
  50.5 14.1 %shard_map.56 = (f32[129,64,128]{2,1,0:T(8,128)}, f32[1024,128]{1,0:T(8,128)}) custom-call(s32[1]{0:T(128)S(6)} %copy.8.kept_ref, s32[256]{0:T(256)} %bitcast.13, s32[256]{0:T(256)} %bitcast.12, s32[128]{0:T(128)} %scatter_custom_fusion.place_ref, bf16[256,64,128]{2,1,0:T(8,128)(2,1)} %get-tuple-element.9.tiles_ref, f32[128,64,128]{2,1,0:T(8,128)} %bitcast.10), custom_call_target="tpu_custom_call" | custom-call | tf_op jit(solution)/shard_map/pallas_call | solution.py:398
  64.5 168.0 %shard_map.57 = f32[512,1024]{1,0:T(8,128)} custom-call(f32[129,64,128]{2,1,0:T(8,128)} %get-tuple-element.11.half_ref, f32[1024,128]{1,0:T(8,128)} %get-tuple-element.12.panel_ref), custom_call_target="tpu_custom_call" | custom-call | tf_op jit(solution)/shard_map/pallas_call | solution.py:411
  232.6 3.2 %copy.9 = f32[8,64,1024]{2,1,0:T(8,128)} copy(f32[8,64,1024]{2,1,0:T(8,128)} %bitcast.9) | data formatting | bytes 4194304
  (1 shorter events, 0.0 us)

commit v3 on v2

--- a/solution.py
+++ b/solution.py
@@ -47,8 +47,9 @@
                 part = products[u][parity * (BLK // 2):(parity + 1) * (BLK // 2)]
                 half_ref[place, pl.ds(parity, BLK // 2, stride=2), :] += part
 
-    for a in range(PBLK):
-        panel_ref[pl.ds(a * BLK, BLK), :] = half_ref[place_ref[a]]
+    for a in range(0, PBLK, 2):
+        pair = jnp.concatenate([half_ref[place_ref[a]], half_ref[place_ref[a + 1]]], axis=0)
+        panel_ref[:, pl.ds(a * BLK, 2 * BLK)] = pair.T
 
 
 def spread_kernel(shape, coefficients_ref, shard_ref, tiles_ref, gathered, z_send, y_send, c_send, recv, local_sem):
@@ -197,8 +198,7 @@
         return (zz * ny + yy) * 2 + cc
 
     def partner(i):
-        k = lax.rem(i // (2 * ny) + nz // 2, nz)
-        return k, lax.rem(i // 2, ny), lax.rem(i, 2)
+        return lax.rem(i + nz // 2, nz), lax.rem(i // (2 * nz), ny), lax.rem(i // nz, 2)
 
     def send_to(i):
         k, dy, dc = partner(i)
@@ -261,13 +261,18 @@
     own_panel.start()
     own_rows.start()
 
-    @pl.loop(0, n)
-    def _(i):
-        dst = send_to(i)
-
-        @pl.when(dst != me)
-        def _():
-            row_copy(dst, me).start()
+    batch = n // nz
+
+    def send_rows(part):
+        @pl.loop(0, batch)
+        def _(j):
+            dst = send_to(part * batch + j)
+
+            @pl.when(dst != me)
+            def _():
+                row_copy(dst, me).start()
+
+    send_rows(0)
 
     def from_y(zz):
         if ny > 1:
@@ -275,7 +280,14 @@
             wait_panel(q)
             panel_copy(q, other_c, c_send.at[q]).start()
 
-    from_y(z)
+    def pair_from_y(d):
+        @pl.when(z - d >= 0)
+        def _():
+            from_y(z - d)
+
+        @pl.when((z + d < nz) & (d > 0))
+        def _():
+            from_y(z + d)
 
     @pl.loop(1, nz)
     def _(d):
@@ -301,13 +313,10 @@
 
             spread(q)
 
-        @pl.when(z - d >= 0)
-        def _():
-            from_y(z - d)
-
-        @pl.when(z + d < nz)
-        def _():
-            from_y(z + d)
+        send_rows(d)
+        pair_from_y(d - 1)
+
+    pair_from_y(nz - 1)
 
     @pl.loop(0, nz * ny)
     def _(j):
@@ -333,11 +342,9 @@
         @pl.loop(0, width // TILE)
         def _(j):
             start = pl.multiple_of(j * TILE, TILE)
-            p_high, p_low = halves(panels[q, pl.ds(start, TILE), :])
-            rhs = jnp.concatenate([p_high, p_low, p_high], axis=1)
-            out_ref[:, pl.ds(start, TILE)] += lax.dot_general(
-                lhs[...], rhs, (((1,), (1,)), ((), ())), preferred_element_type=jnp.float32
-            )
+            p_high, p_low = halves(panels[q, :, pl.ds(start, TILE)])
+            rhs = jnp.concatenate([p_high, p_low, p_high], axis=0)
+            out_ref[:, pl.ds(start, TILE)] += jnp.dot(lhs[...], rhs, preferred_element_type=jnp.float32)
 
     @pl.loop(0, n)
     def _(i):
@@ -399,7 +406,7 @@
         functools.partial(half_kernel, block_count),
         out_shape=(
             jax.ShapeDtypeStruct((block_count + 1, BLK, LANES), jnp.float32),
-            jax.ShapeDtypeStruct((width, LANES), jnp.float32),
+            jax.ShapeDtypeStruct((LANES, width), jnp.float32),
         ),
         in_specs=[smem] * 4 + [vmem] * 2,
         out_specs=(vmem, vmem),
@@ -415,7 +422,7 @@
         out_specs=vmem,
         scratch_shapes=[
             pltpu.VMEM((n, owned, BLK, LANES), jnp.float32),
-            pltpu.VMEM((n, width, LANES), jnp.float32),
+            pltpu.VMEM((n, LANES, width), jnp.float32),
             pltpu.VMEM((rows, 3 * LANES), jnp.bfloat16),
             dma((n,)), dma((n,)), dma((2, n)), dma((n,)), dma((n,)), dma((n,)), dma((2,)),
         ],

time: 236 us -> 221 us (0.936)
  Pallas kernels: 222 us -> 207 us
    pallas_call x1, Pallas kernels: 168 us -> 154 us  [shards(): pl.pallas_call(functools.partial(exchange_kernel, (nz, ny, n)), out_shape...]
where the time goes in v3:
time: 221 us
  Pallas kernels  207 us (94%)
  local copies, waits for them, and re-layouts  12.4 us (6%)
    pallas_call x1, Pallas kernels, shards(): pl.pallas_call(functools.partial(exchange_kernel, (nz, ny, n)), out_shape...  154 us
    pallas_call x1, Pallas kernels, shards(): pl.pallas_call(functools.partial(spread_kernel, (nz, ny, n)), out_shape=(...  39.9 us
    pallas_call x1, Pallas kernels, shards(): pl.pallas_call(functools.partial(half_kernel, block_count), out_shape=(ja...  13.4 us
    unnamed x2, local copies, waits for them, and re-layouts  8.03 us

profile of v3, /device:TPU:1, one launch (start us, length us, event | category | flops | bytes accessed | tf_op | source)
XLA Modules:
  0.0 220.8 jit_solution(15527001350409062875)
XLA Ops:
  0.7 0.7 compare_select_fusion
  1.3 1.4 scatter_custom_fusion.place_ref
  2.8 1.2 fusion.2
  4.0 1.7 pad.4.shard_ref
  5.7 4.9 %copy.6 = f32[32,8,32,128]{3,2,1,0:T(8,128)} copy(f32[32,8,32,128]{3,1,2,0:T(8,128)} %bitcast.11) | data formatting | bytes 8388608
  10.5 39.9 %shard_map.55 = (bf16[256,64,128]{2,1,0:T(8,128)(2,1)}, f32[16,512,128]{2,1,0:T(8,128)}) custom-call(f32[256,32,128]{2,1,0:T(8,128)} %bitcast.8, f32[512,128]{1,0:T(8,128)} %pad.4.shard_ref), custom_call_target="tpu_custom_call" | custom-call | tf_op jit(solution)/shard_map/pallas_call | solution.py:394
  50.5 13.4 %shard_map.56 = (f32[129,64,128]{2,1,0:T(8,128)}, f32[128,1024]{1,0:T(8,128)}) custom-call(s32[1]{0:T(128)S(6)} %copy.8.kept_ref, s32[256]{0:T(256)} %bitcast.13, s32[256]{0:T(256)} %bitcast.12, s32[128]{0:T(128)} %scatter_custom_fusion.place_ref, bf16[256,64,128]{2,1,0:T(8,128)(2,1)} %get-tuple-element.9.tiles_ref, f32[128,64,128]{2,1,0:T(8,128)} %bitcast.10), custom_call_target="tpu_custom_call" | custom-call | tf_op jit(solution)/shard_map/pallas_call | solution.py:405
  63.8 153.8 %shard_map.57 = f32[512,1024]{1,0:T(8,128)} custom-call(f32[129,64,128]{2,1,0:T(8,128)} %get-tuple-element.11.half_ref, f32[128,1024]{1,0:T(8,128)} %get-tuple-element.12.panel_ref), custom_call_target="tpu_custom_call" | custom-call | tf_op jit(solution)/shard_map/pallas_call | solution.py:418
  217.6 3.2 %copy.9 = f32[8,64,1024]{2,1,0:T(8,128)} copy(f32[8,64,1024]{2,1,0:T(8,128)} %bitcast.9) | data formatting | bytes 4194304
  (1 shorter events, 0.0 us)
